TPU v7x, 32 devices: a whole 2x2x4 slice. The times are simulated.
32 devices in a mesh: groups: 1, dp: 32 (over z, y, x, core).
Axes of the slice: x: 2, y: 2, z: 4, core: 2. Of those that a mesh axis runs over, the one named last changes fastest.
Arguments:
- x_in: bfloat16 [2048, 4096], P('groups', 'dp'), may hold values from -6 to 6
- z_in: bfloat16 [2048, 4096], P('groups', 'dp'), may hold values from -6 to 6
- dt_in: bfloat16 [64, 2048], P('dp', 'groups'), may hold values from -2.5 to 7.5
- bc_in: bfloat16 [8, 2048, 512], P(None, ('groups', 'dp')), may hold values from -6 to 6
- owner_states: float32 [32, 1, 64, 8, 256], P(('groups', 'dp')), may hold values from -1.75 to 1.75
- decay_rate: float32 [64], P('dp'), may hold values from 0.0001 to 1
- dt_bias: float32 [64], P('dp'), may hold values from -4.5 to -2.5
- skip_d: float32 [64], P('dp'), may hold values from 0.5 to 1.5
- norm_gain: float32 [4096], P('dp'), may hold values from 0.5 to 1.5
- owner_map: int32 [4], P('groups'), may hold values from 0 to 3, each once
- prefill_slot: int32 [4], P('groups'), may hold values from 0 to 3, each once
- turn_blocks: int32 [4], P('groups'), may hold values from 1 to 8, 16 in all
Outputs:
- y_out: bfloat16 [2048, 4096], P('groups', 'dp')
- new_owner_states: float32 [32, 1, 64, 8, 256], P(('groups', 'dp'))
Inputs may be any that keep to these rules, and one draw needn't show every extreme that they name: `owner_map`: a permutation; slot k belongs to decode owner k. `prefill_slot`: a permutation. `turn_blocks`: sums to 16; a turn of b blocks has b * 128 tokens.
All inputs are finite; a program needn't handle non-finite values.
Results may differ from a plain program's by a relative error of at most 0.0055.
Values may be sent and summed in bfloat16 or wider, within the bound.
A program may use at most 128 MiB of HBM per device.

v0:
```python
import jax
import jax.numpy as jnp
from jax import lax
from jax.sharding import PartitionSpec as P

BLOCK_LEN = 128


exact_mode = lax.Precision.HIGHEST


def shortened(x):

    def short(part):
        return part.astype(jnp.bfloat16) if part.dtype == jnp.float32 else part

    return jax.tree.map(short, x)


def from_partner(x, axis, bit):
    return lax.ppermute(x, axis, [(i, i ^ 1 << bit) for i in range(lax.axis_size(axis))])


def packing(prefill_slot, turn_blocks, block_total):
    conv_count = turn_blocks.shape[0]
    conv_ids = jnp.arange(conv_count, dtype=jnp.int32)
    before_mask = (prefill_slot[None, :] < prefill_slot[:, None]).astype(jnp.int32)
    first_block = jnp.sum(before_mask * turn_blocks[None, :], axis=1)
    end_block = first_block + turn_blocks
    block_ids = jnp.arange(block_total, dtype=jnp.int32)
    inside_mask = (block_ids[:, None] >= first_block[None, :]) & (
        block_ids[:, None] < end_block[None, :]
    )
    block_conv = jnp.sum(jnp.where(inside_mask, conv_ids[None, :], 0), axis=1)
    return (first_block, end_block, block_conv)


def fetch_states(owner_states):
    return lax.all_to_all(
        owner_states[0].astype(jnp.bfloat16), "dp", split_axis=1, concat_axis=2, tiled=True
    ).astype(jnp.float32)


def shards(
    x_in,
    z_in,
    dt_in,
    bc_in,
    owner_states,
    decay_rate,
    dt_bias,
    skip_d,
    norm_gain,
    owner_map,
    prefill_slot,
    turn_blocks,
):
    device_count = lax.axis_size("dp")
    token_count = x_in.shape[0]
    head_local = dt_in.shape[0]
    head_width = x_in.shape[1] // head_local
    group_count = bc_in.shape[0]
    state_width = bc_in.shape[2] // 2
    slot_count = owner_states.shape[1]
    channel_part = owner_states.shape[3]
    decode_width = head_width // channel_part
    owner_count = device_count // decode_width
    block_count = token_count // BLOCK_LEN
    conv_count = owner_map.shape[0]
    per_group = device_count // group_count
    first_block, end_block, block_conv = packing(prefill_slot, turn_blocks, block_count)
    slot_of = owner_map % slot_count
    owner_of = owner_map // slot_count
    copies = jnp.repeat(bc_in, per_group, axis=0)
    bc_group = lax.all_to_all(copies, "dp", split_axis=0, concat_axis=1, tiled=True)[0]
    b_part = bc_group[:, :state_width].reshape(block_count, BLOCK_LEN, state_width)
    c_part = bc_group[:, state_width:].reshape(block_count, BLOCK_LEN, state_width)
    c_float = c_part.astype(jnp.float32)
    step_size = jax.nn.softplus(dt_in.astype(jnp.float32) + dt_bias[:, None])
    log_decay = -step_size * decay_rate[:, None]
    cum_decay = jnp.cumsum(log_decay.reshape(head_local, block_count, BLOCK_LEN), axis=2)
    step_blocks = step_size.reshape(head_local, block_count, BLOCK_LEN)
    block_decay = cum_decay[:, :, -1]
    value_blocks = x_in.reshape(block_count, BLOCK_LEN, head_local, head_width)
    gate_blocks = z_in.reshape(block_count, BLOCK_LEN, head_local, head_width)
    scores = jnp.einsum("kts,kus->ktu", c_part, b_part, preferred_element_type=jnp.float32)
    causal = jnp.arange(BLOCK_LEN)[:, None] >= jnp.arange(BLOCK_LEN)[None, :]
    log_gap = cum_decay[:, :, :, None] - cum_decay[:, :, None, :]
    pair_decay = jnp.exp(jnp.where(causal[None, None], log_gap, -jnp.inf))
    weights = (scores[None] * pair_decay * step_blocks[:, :, None, :]).astype(jnp.bfloat16)
    local_out = jnp.einsum(
        "hktu,kuhp->kthp", weights, value_blocks, preferred_element_type=jnp.float32
    )
    tail_scale = jnp.transpose(
        step_blocks * jnp.exp(block_decay[:, :, None] - cum_decay), (1, 2, 0)
    )
    carried = (value_blocks * tail_scale[..., None]).astype(jnp.bfloat16)
    block_input = jnp.einsum("kuhp,kus->khps", carried, b_part, preferred_element_type=jnp.float32)
    block_ids = jnp.arange(block_count, dtype=jnp.int32)
    target_end = jnp.concatenate([block_ids, end_block])
    target_conv = jnp.concatenate([block_conv, jnp.arange(conv_count, dtype=jnp.int32)])
    destination_first = first_block[target_conv]
    link_mask = (block_conv[None, :] == target_conv[:, None]) & (
        block_ids[None, :] < target_end[:, None]
    )
    lead_sum = jnp.concatenate(
        [jnp.zeros((head_local, 1), jnp.float32), jnp.cumsum(block_decay, axis=1)], axis=1
    )
    lead_end = lead_sum[:, target_end]
    carry_weight = jnp.exp(
        jnp.where(link_mask[None], lead_end[:, :, None] - lead_sum[:, None, 1:], -jnp.inf)
    )
    seed_weight = jnp.exp(lead_end - lead_sum[:, destination_first])
    zero_part = jnp.einsum("hrj,jhps->rhps", carry_weight, block_input, precision=exact_mode)
    decay_factor = jnp.transpose(jnp.exp(cum_decay), (1, 2, 0))[..., None]
    shaped = fetch_states(owner_states).reshape(
        slot_count, head_local, owner_count, head_width, state_width
    )
    initial = shaped[slot_of, :, owner_of]
    boundary = zero_part + jnp.transpose(seed_weight)[:, :, None, None] * initial[target_conv]
    state_out = decay_factor * jnp.einsum(
        "kts,khps->kthp", c_float, boundary[:block_count], precision=exact_mode
    )
    final_state = boundary[block_count:]
    mixer_out = local_out + state_out + skip_d[None, None, :, None] * value_blocks
    gated = mixer_out * jax.nn.silu(gate_blocks.astype(jnp.float32))
    gated_rows = gated.reshape(token_count, head_local * head_width)
    part_square = jnp.sum(gated_rows * gated_rows, axis=1)
    group_square = part_square
    for bit_index in range(per_group.bit_length() - 1):
        group_square = group_square + from_partner(shortened(group_square), "dp", bit_index).astype(
            group_square.dtype
        )
    mean_square = group_square / (per_group * head_local * head_width)
    y_out = (gated_rows * lax.rsqrt(mean_square + 1e-05)[:, None] * norm_gain[None, :]).astype(
        jnp.bfloat16
    )
    blank_slots = jnp.zeros(
        (slot_count, head_local, owner_count, head_width, state_width), jnp.float32
    )
    filled = blank_slots.at[slot_of, :, owner_of].set(final_state)
    outgoing = filled.reshape(slot_count, head_local, owner_count * head_width, state_width)
    returned = lax.all_to_all(outgoing, "dp", split_axis=2, concat_axis=1, tiled=True)
    return (y_out, returned[None])


def solution(mesh):
    placed = (
        P("groups", "dp"),
        P("groups", "dp"),
        P("dp", "groups"),
        P(None, ("groups", "dp"), None),
        P(("groups", "dp"), None, None, None, None),
        P("dp"),
        P("dp"),
        P("dp"),
        P("dp"),
        P("groups"),
        P("groups"),
        P("groups"),
    )
    return jax.shard_map(
        shards,
        mesh=mesh,
        in_specs=placed,
        out_specs=(P("groups", "dp"), P(("groups", "dp"), None, None, None, None)),
        check_vma=False,
    )
```

profile of v0, /device:TPU:0, one launch (start us, length us, event | category | flops | bytes accessed | tf_op | source)
XLA Modules:
  0.0 108.3 jit_solution(3293635196521306495)
XLA Ops:
  0.6 1.1 convert_bitcast_fusion.1
  1.7 17.7 %all_to_all.33 = bf16[1,64,8,256]{3,2,0,1:T(8,128)(2,1)S(1)} all-to-all(bf16[1,64,8,256]{3,2,0,1:T(8,128)(2,1)S(1)} %convert_bitcast_fusion.1), channel_id=1, replica_groups=mesh['groups'=1,'dp'=32] {'dp'}, dimensions={1} | all-to-all | bytes 524288 | tf_op jit(solution)/shard_map/all_to_all | solution.py:39
  19.4 2.6 %broadcast_in_dim.40 = bf16[8,4,64,512]{3,2,1,0:T(8,128)(2,1)} broadcast(bf16[8,64,512]{2,1,0:T(8,128)(2,1)} %param.15), dimensions={0,2,3} | broadcast | bytes 2621440 | tf_op jit(solution)/shard_map/broadcast_in_dim | solution.py:74
  22.0 0.0 copy-start.12
  22.0 0.0 copy-start.7
  22.0 3.6 %all-to-all-start = ((bf16[32,64,512]{2,1,0:T(8,128)(2,1)}), bf16[32,64,512]{2,1,0:T(8,128)(2,1)}, u32[]{:S(2)}, u32[]{:S(2)}) async-start(bf16[32,64,512]{2,1,0:T(8,128)(2,1)} %bitcast), calls=%async_computation | async-start | bytes 4194304 | tf_op jit(solution)/shard_map/all_to_all | solution.py:75
  25.7 0.0 copy-done.10
  25.7 0.0 copy-done.14
  25.7 0.0 copy-start.8
  25.7 0.2 select_reduce_fusion.1
  25.9 0.0 copy-done.11
  25.9 0.0 copy-done.12
  25.9 0.1 multiply_bitcast_fusion
  26.1 0.6 reduce_window_sum.22
  26.7 0.2 slice_reduce_fusion
  26.8 0.2 reduce_window_sum.23
  27.0 0.1 copy.126
  27.1 0.6 fusion.55
  27.7 0.1 select_reduce_fusion
  27.8 2.5 %fusion.50 = (s32[20]{0:T(128)S(1)}, s32[20]{0:T(128)S(1)}) fusion(s32[]{:T(128)} %bitcast.18, s32[]{:T(128)} %bitcast.19, s32[]{:T(128)} %bitcast.20, s32[]{:T(128)} %bitcast.21, s32[4,1]{0,1:T(1,128)S(1)} %iota.81, s32[16,1]{0,1:T(1,128)S(1)} %bitcast.127), kind=kLoop, calls=%fused_computation.79 | loop fusion | flops 260 | bytes 256 | tf_op jit(solution)/shard_map/select_n | solution.py:113
  30.3 0.6 gather_fusion.1
  30.9 0.1 fusion.48
  31.0 0.6 gather_fusion
  31.5 0.1 copy.105
  31.6 0.1 exponential_bitcast_fusion
  31.7 0.4 reshape.361
  32.1 1.8 %copy.97 = bf16[16,128,2,64]{1,3,2,0:T(8,128)(2,1)} copy(bf16[16,128,2,64]{3,2,1,0:T(2,128)(2,1)S(1)} %reshape.361) | data formatting | bytes 1048576 | tf_op jit(solution)/shard_map/reshape | solution.py:84
  33.9 0.1 copy.102
  34.0 1.1 %reshape.362 = f32[16,128,2,64]{3,2,1,0:T(2,128)S(1)} reshape(bf16[2048,128]{1,0:T(8,128)(2,1)S(1)} %copy-done.8) | data formatting | bytes 1572864 | tf_op jit(solution)/shard_map/convert_element_type | solution.py:126
  35.2 0.0 copy-start.15
  35.2 2.1 %copy.112 = f32[16,128,2,64]{1,3,2,0:T(8,128)} copy(f32[16,128,2,64]{3,2,1,0:T(2,128)S(1)} %reshape.362) | data formatting | bytes 2097152 | tf_op jit(solution)/shard_map/convert_element_type | solution.py:126
  37.3 0.1 pad_add_fusion
  37.4 0.1 fusion.43
  37.6 0.6 gather_fusion.2
  38.2 0.7 gather_fusion.3
  38.9 35.7 %all-to-all-done = bf16[32,64,512]{2,1,0:T(8,128)(2,1)} async-done(((bf16[32,64,512]{2,1,0:T(8,128)(2,1)}), bf16[32,64,512]{2,1,0:T(8,128)(2,1)}, u32[]{:S(2)}, u32[]{:S(2)}) %all-to-all-start) | async-done | bytes 2097184 | tf_op jit(solution)/shard_map/all_to_all | solution.py:75
  74.6 2.7 %fusion.54 = (bf16[2048,256]{1,0:T(8,128)(2,1)S(1)}, bf16[2048,256]{1,0:T(8,128)(2,1)}) fusion(bf16[2048,512]{1,0:T(8,128)(2,1)} %bitcast.1), kind=kLoop, calls=%fused_computation.85 | loop fusion | bytes 4194304 | tf_op jit(solution)/shard_map/slice | solution.py:76
  77.3 1.0 copy-done.1
  78.3 0.4 fusion.30
  78.8 5.4 %bitcast_add_fusion = f32[20,2,64,256]{3,0,2,1:T(8,128)S(1)} fusion(f32[20,2,64,256]{3,2,1,0:T(8,128)S(1)} %gather_fusion.3, f32[16,2,64,256]{3,2,1,0:T(8,128)S(1)} %fusion.30, f32[20,2]{0,1:T(2,128)S(1)} %copy.105, f32[2,16]{1,0:T(2,128)S(1)} %reduce_window_sum.23, f32[2,20]{1,0:T(2,128)S(1)} %copy.102, pred[20,16]{0,1:T(8,128)(4,1)S(1)} %fusion.43), kind=kOutput, calls=%fused_computation.5 | convolution fusion | flops 127141120 | bytes 7340800 | tf_op jit(solution)/shard_map/hrj,jhps->rhps/dot_general | solution.py:114
  84.1 0.0 copy-start
  84.1 1.6 %copy-done = f32[20,2,64,256]{3,0,2,1:T(8,128)} copy-done((f32[20,2,64,256]{3,0,2,1:T(8,128)}, f32[20,2,64,256]{3,0,2,1:T(8,128)S(1)}, u32[]{:S(2)}) %copy-start) | copy-done | bytes 2621464
  85.8 0.1 slice.39
  85.8 0.1 copy.114
  86.0 0.7 scatter_fusion
  86.8 1.2 %copy.115 = f32[1,2,256,256]{3,1,0,2:T(2,128)} copy(f32[1,2,256,256]{3,2,1,0:T(8,128)S(1)} %bitcast.115) | data formatting | bytes 1048576 | tf_op jit(solution)/shard_map/reshape | solution.py:142
  88.0 4.0 %all-to-all-start.2 = ((f32[1,2,256,256]{3,1,0,2:T(2,128)}), f32[1,2,256,256]{3,1,0,2:T(2,128)S(1)}, u32[]{:S(2)}, u32[]{:S(2)}) async-start(f32[1,2,256,256]{3,1,0,2:T(2,128)} %copy.115), calls=%async_computation.2 | async-start | bytes 1048576 | tf_op jit(solution)/shard_map/all_to_all | solution.py:143
  92.0 0.4 fusion.56
  92.5 0.0 slice-start
  92.5 0.0 copy-start.16
  92.5 0.9 convolution_bitcast_fusion
  93.4 0.6 slice-done
  94.1 0.3 copy-done.6
  94.3 2.6 %multiply_reduce_fusion = (f32[16,128]{1,0:T(8,128)S(1)}, f32[16,128,2,64]{1,3,2,0:T(8,128)S(1)}) fusion(f32[16,128,2,64]{1,3,2,0:T(8,128)S(1)} %copy-done.6, bf16[16,128,2,64]{1,3,2,0:T(8,128)(2,1)S(1)} %copy-done.5, f32[2]{0:T(128)S(1)} %copy-done.16, f32[16,128,2,64]{1,3,2,0:T(8,128)S(1)} %convolution_bitcast_fusion, ...), kind=kOutput, calls=%fused_computation.24 | convolution fusion | flops 808450048 | bytes 6840328 | tf_op jit(solution)/shard_map/kts,khps->kthp/dot_general | solution.py:121
  97.0 0.0 copy-start.13
  97.0 0.1 collective-permute-start
  97.1 1.1 %collective-permute-done = bf16[2048]{0:T(1024)(128)(2,1)S(1)} collective-permute-done((bf16[2048]{0:T(1024)(128)(2,1)S(1)}, bf16[2048]{0:T(1024)(128)(2,1)S(1)}, u32[]{:S(2)}, u32[]{:S(2)}) %collective-permute-start) | collective-permute-done | bytes 4128 | tf_op jit(solution)/shard_map/ppermute | solution.py:21
  98.2 1.6 %collective-permute-start.1 = (bf16[2048]{0:T(1024)(128)(2,1)S(1)}, bf16[2048]{0:T(1024)(128)(2,1)S(1)}, u32[]{:S(2)}, u32[]{:S(2)}) collective-permute-start(bf16[2048]{0:T(1024)(128)(2,1)S(1)} %fusion.45), channel_id=1, source_target_pairs={{0,2},{1,3},{2,0},{3,1},{4,6},{5,7},{6,4},{7,5},{8,10},{9,11},{10,... | collective-permute-start | bytes 12296 | tf_op jit(solution)/shard_map/ppermute | solution.py:21
  99.8 0.6 copy.113
  100.4 1.4 %collective-permute-done.1 = bf16[2048]{0:T(1024)(128)(2,1)S(1)} collective-permute-done((bf16[2048]{0:T(1024)(128)(2,1)S(1)}, bf16[2048]{0:T(1024)(128)(2,1)S(1)}, u32[]{:S(2)}, u32[]{:S(2)}) %collective-permute-start.1) | collective-permute-done | bytes 4128 | tf_op jit(solution)/shard_map/ppermute | solution.py:21
  101.9 0.4 fusion.23
  102.3 1.0 copy.118
  103.3 4.1 %all-to-all-done.2 = f32[1,2,256,256]{3,1,0,2:T(2,128)S(1)} async-done(((f32[1,2,256,256]{3,1,0,2:T(2,128)}), f32[1,2,256,256]{3,1,0,2:T(2,128)S(1)}, u32[]{:S(2)}, u32[]{:S(2)}) %all-to-all-start.2) | async-done | bytes 524320 | tf_op jit(solution)/shard_map/all_to_all | solution.py:143
  107.4 0.9 copy.117
  (42 shorter events, 0.3 us)
Async XLA Ops:
  22.0 3.7 %copy-start.10 = (s32[4]{0:T(128)S(1)}, s32[4]{0:T(128)}, u32[]{:S(2)}) copy-start(s32[4]{0:T(128)} %param.22) | copy-start | bytes 52
  22.0 3.7 %copy-start.14 = (s32[4]{0:T(128)S(1)}, s32[4]{0:T(128)}, u32[]{:S(2)}) copy-start(s32[4]{0:T(128)} %param.23) | copy-start | bytes 52
  22.0 3.9 %copy-start.9 = (bf16[2,2048]{1,0:T(2,128)(2,1)S(1)}, bf16[2,2048]{1,0:T(2,128)(2,1)}, u32[]{:S(2)}) copy-start(bf16[2,2048]{1,0:T(2,128)(2,1)} %param.14) | copy-start | bytes 24580
  22.0 3.9 %copy-start.11 = (f32[2]{0:T(128)S(1)}, f32[2]{0:T(128)}, u32[]{:S(2)}) copy-start(f32[2]{0:T(128)} %param.17) | copy-start | bytes 28
  22.0 3.9 %copy-start.12 = (f32[2]{0:T(128)S(1)}, f32[2]{0:T(128)}, u32[]{:S(2)}) copy-start(f32[2]{0:T(128)} %param.18) | copy-start | bytes 28
  22.0 9.7 %copy-start.7 = (bf16[2048,128]{1,0:T(8,128)(2,1)S(1)}, bf16[2048,128]{1,0:T(8,128)(2,1)}, u32[]{:S(2)}) copy-start(bf16[2048,128]{1,0:T(8,128)(2,1)} %param.12) | copy-start | bytes 1572868
  22.0 52.5 %all-to-all-start = ((bf16[32,64,512]{2,1,0:T(8,128)(2,1)}), bf16[32,64,512]{2,1,0:T(8,128)(2,1)}, u32[]{:S(2)}, u32[]{:S(2)}) async-start(bf16[32,64,512]{2,1,0:T(8,128)(2,1)} %bitcast), calls=%async_computation | async-start | bytes 4194304 | tf_op jit(solution)/shard_map/all_to_all | solution.py:75
  25.7 8.3 %copy-start.8 = (bf16[2048,128]{1,0:T(8,128)(2,1)S(1)}, bf16[2048,128]{1,0:T(8,128)(2,1)}, u32[]{:S(2)}) copy-start(bf16[2048,128]{1,0:T(8,128)(2,1)} %param.13) | copy-start | bytes 1572868
  35.2 2.2 %copy-start.15 = (s32[4]{0:T(128)S(1)}, s32[4]{0:T(128)}, u32[]{:S(2)}) copy-start(s32[4]{0:T(128)} %param.21) | copy-start | bytes 52
  74.6 3.7 %copy-start.4 = (bf16[16,128,2,64]{1,3,2,0:T(8,128)(2,1)S(1)}, bf16[16,128,2,64]{1,3,2,0:T(8,128)(2,1)}, u32[]{:S(2)}) copy-start(bf16[16,128,2,64]{1,3,2,0:T(8,128)(2,1)} %copy.97) | copy-start | bytes 1572868
  77.3 1.0 copy-start.1
  84.1 1.6 %copy-start = (f32[20,2,64,256]{3,0,2,1:T(8,128)}, f32[20,2,64,256]{3,0,2,1:T(8,128)S(1)}, u32[]{:S(2)}) copy-start(f32[20,2,64,256]{3,0,2,1:T(8,128)S(1)} %bitcast_add_fusion) | copy-start | bytes 7864324
  86.0 6.1 %copy-start.2 = (bf16[2048,256]{1,0:T(8,128)(2,1)S(1)}, bf16[2048,256]{1,0:T(8,128)(2,1)}, u32[]{:S(2)}) copy-start(bf16[2048,256]{1,0:T(8,128)(2,1)} %copy-done.1) | copy-start | bytes 3145732
  86.0 6.1 %copy-start.3 = (bf16[2048,256]{1,0:T(8,128)(2,1)S(1)}, bf16[2048,256]{1,0:T(8,128)(2,1)}, u32[]{:S(2)}) copy-start(bf16[2048,256]{1,0:T(8,128)(2,1)} %get-tuple-element.15) | copy-start | bytes 3145732
  88.0 4.5 %copy-start.5 = (bf16[16,128,2,64]{1,3,2,0:T(8,128)(2,1)S(1)}, bf16[16,128,2,64]{1,3,2,0:T(8,128)(2,1)}, u32[]{:S(2)}) copy-start(bf16[16,128,2,64]{1,3,2,0:T(8,128)(2,1)} %copy.97) | copy-start | bytes 1572868
  88.0 19.4 %all-to-all-start.2 = ((f32[1,2,256,256]{3,1,0,2:T(2,128)}), f32[1,2,256,256]{3,1,0,2:T(2,128)S(1)}, u32[]{:S(2)}, u32[]{:S(2)}) async-start(f32[1,2,256,256]{3,1,0,2:T(2,128)} %copy.115), calls=%async_computation.2 | async-start | bytes 1048576 | tf_op jit(solution)/shard_map/all_to_all | solution.py:143
  92.5 1.6 %slice-start = ((f32[20,2,64,256]{3,0,2,1:T(8,128)}), f32[16,2,64,256]{3,0,2,1:T(8,128)S(1)}, s32[]{:S(2)}) async-start(f32[20,2,64,256]{3,0,2,1:T(8,128)} %copy-done), calls=%async_computation.3 | async-start | bytes 4194304 | tf_op jit(solution)/shard_map/slice | solution.py:122
  92.5 1.8 %copy-start.6 = (f32[16,128,2,64]{1,3,2,0:T(8,128)S(1)}, f32[16,128,2,64]{1,3,2,0:T(8,128)}, u32[]{:S(2)}) copy-start(f32[16,128,2,64]{1,3,2,0:T(8,128)} %copy.112) | copy-start | bytes 3145732
  92.5 1.8 %copy-start.16 = (f32[2]{0:T(128)S(1)}, f32[2]{0:T(128)}, u32[]{:S(2)}) copy-start(f32[2]{0:T(128)} %param.19) | copy-start | bytes 28
  97.0 4.9 %copy-start.13 = (f32[128]{0:T(128)S(1)}, f32[128]{0:T(128)}, u32[]{:S(2)}) copy-start(f32[128]{0:T(128)} %param.20) | copy-start | bytes 1540
  97.0 1.2 %collective-permute-start = (bf16[2048]{0:T(1024)(128)(2,1)S(1)}, bf16[2048]{0:T(1024)(128)(2,1)S(1)}, u32[]{:S(2)}, u32[]{:S(2)}) collective-permute-start(bf16[2048]{0:T(1024)(128)(2,1)S(1)} %bitcast_convert_fusion), channel_id=1, source_target_pairs={{0,1},{1,0},{2,3},{3,2},{4,5},{5,4},{6,7},{7,6},{8,9},{9,8},{10,11... | collective-permute-start | bytes 12296 | tf_op jit(solution)/shard_map/ppermute | solution.py:21
  98.2 3.6 %collective-permute-start.1 = (bf16[2048]{0:T(1024)(128)(2,1)S(1)}, bf16[2048]{0:T(1024)(128)(2,1)S(1)}, u32[]{:S(2)}, u32[]{:S(2)}) collective-permute-start(bf16[2048]{0:T(1024)(128)(2,1)S(1)} %fusion.45), channel_id=1, source_target_pairs={{0,2},{1,3},{2,0},{3,1},{4,6},{5,7},{6,4},{7,5},{8,10},{9,11},{10,... | collective-permute-start | bytes 12296 | tf_op jit(solution)/shard_map/ppermute | solution.py:21
where the time goes:
time: 109 us; the launch traced here: 108 us
  waiting for transfers between devices  42.3 us (39%)
  local copies, waits for them, and re-layouts  22.5 us (21%)
  blocking collectives  17.7 us (16%)
  matrix products  9.77 us (9%)
  starting transfers between devices  9.41 us (9%)
  other arithmetic  5.59 us (5%)
    all_to_all x1, waiting for transfers between devices, shards(): lax.all_to_all(copies, 'dp', split_axis=0, concat_axis=1, tiled=True)[0]  35.7 us
    all_to_all x1, blocking collectives, fetch_states(): lax.all_to_all(owner_states[0].astype(jnp.bfloat16), 'dp', split_axis=1,...  17.7 us
    dot_general x1, matrix products, shards(): jnp.einsum('hrj,jhps->rhps', carry_weight, block_input, precision=exact_m...  5.38 us
    all_to_all x1, waiting for transfers between devices, shards(): lax.all_to_all(outgoing, 'dp', split_axis=2, concat_axis=1, tiled=True)  4.08 us
    unnamed x37, local copies, waits for them, and re-layouts  4.06 us
    all_to_all x1, starting transfers between devices, shards(): lax.all_to_all(outgoing, 'dp', split_axis=2, concat_axis=1, tiled=True)  4.05 us
    all_to_all x1, starting transfers between devices, shards(): lax.all_to_all(copies, 'dp', split_axis=0, concat_axis=1, tiled=True)[0]  3.63 us
    convert_element_type x2, local copies, waits for them, and re-layouts, shards(): gated = mixer_out * jax.nn.silu(gate_blocks.astype(jnp.float32))  3.24 us
  transfers between devices with their start and end apart: 4, of which 4 were waited for; matrix products, arithmetic and copies ran while one was open for 18% of the time, Pallas kernels for 0%

commit v1 on v0

--- a/solution.py
+++ b/solution.py
@@ -1,6 +1,10 @@
+import functools
+
 import jax
 import jax.numpy as jnp
 from jax import lax
+from jax.experimental import pallas as pl
+from jax.experimental.pallas import tpu as pltpu
 from jax.sharding import PartitionSpec as P
 
 BLOCK_LEN = 128
@@ -144,6 +148,461 @@
     return (y_out, returned[None])
 
 
+def lanes_dot(a, b):
+    return lax.dot_general(a, b, (((1,), (1,)), ((), ())), preferred_element_type=jnp.float32)
+
+
+def rows_dot(a, b):
+    return lax.dot_general(a, b, (((0,), (0,)), ((), ())), preferred_element_type=jnp.float32)
+
+
+def layer_kernel(
+    devices,
+    blocks,
+    owners,
+    om_ref,
+    ps_ref,
+    tb_ref,
+    bias_ref,
+    rate_ref,
+    skip_ref,
+    x_ref,
+    z_ref,
+    dt_ref,
+    bc_ref,
+    st_ref,
+    gain_ref,
+    y_ref,
+    ns_ref,
+    b_buf,
+    c_buf,
+    s_out,
+    s_in,
+    f_out,
+    f_in,
+    sq_out,
+    sq_in,
+    seeds,
+    pair,
+    grow,
+    added,
+    starts,
+    carried,
+    gated,
+    rows_scr,
+    cols_scr,
+    edge_scr,
+    near_send,
+    near_recv,
+    side_send,
+    side_recv,
+    twin_send,
+    twin_recv,
+    last_send,
+    last_recv,
+    init_send,
+    init_recv,
+    fin_send,
+    fin_recv,
+    sq_send,
+    sq_recv,
+):
+    me = lax.axis_index("dp")
+    L = BLOCK_LEN
+    quads = devices // 4
+    quad = me // 4
+    spot = me % 4
+    twin = me + 1 - 2 * (me % 2)
+    side = me + 2 - 4 * ((me // 2) % 2)
+    twin_spot, side_spot = twin % 4, side % 4
+    diag_spot = 3 - spot
+    width = b_buf.shape[1]
+    bufs = (b_buf, c_buf)
+    tokens = bc_ref.shape[1]
+
+    def remote(src, dst, send, recv, to):
+        return pltpu.make_async_remote_copy(
+            src_ref=src,
+            dst_ref=dst,
+            send_sem=send,
+            recv_sem=recv,
+            device_id={"dp": to},
+            device_id_type=pl.DeviceIdType.MESH,
+        )
+
+    def chunk(k, q, s):
+        return bufs[k].at[pl.ds(pl.multiple_of((4 * q + s) * tokens, tokens), tokens), :]
+
+    def near(k, q):
+        return remote(
+            bc_ref.at[q, :, k * width : (k + 1) * width],
+            chunk(k, quad, spot),
+            near_send.at[k, q],
+            near_recv.at[k, quad],
+            4 * q + spot,
+        )
+
+    def near_in(k, q):
+        return remote(
+            chunk(k, q, spot), chunk(k, q, spot), near_send.at[k, q], near_recv.at[k, q], side
+        )
+
+    def to_side(k, q, s):
+        return remote(chunk(k, q, s), chunk(k, q, s), side_send.at[k, q], side_recv.at[k, q], side)
+
+    def to_twin(k, q, s):
+        return remote(chunk(k, q, s), chunk(k, q, s), twin_send.at[k, q], twin_recv.at[k, q], twin)
+
+    def to_twin_last(k, q, s):
+        return remote(chunk(k, q, s), chunk(k, q, s), last_send.at[k, q], last_recv.at[k, q], twin)
+
+    def init_copy(d):
+        return remote(s_out.at[d], s_in.at[me], init_send.at[d], init_recv.at[me], d)
+
+    def init_from(d):
+        return remote(s_in.at[d], s_in.at[d], init_send.at[d], init_recv.at[d], side)
+
+    def fin_copy(d):
+        return remote(f_out.at[d], f_in.at[me], fin_send.at[d], fin_recv.at[me], d)
+
+    def fin_from(d):
+        return remote(f_in.at[d], f_in.at[d], fin_send.at[d], fin_recv.at[d], side)
+
+    def every(count, body):
+        lax.fori_loop(0, count, lambda i, c: (body(i), c)[1], 0)
+
+    barrier = pltpu.get_barrier_semaphore()
+
+    def greet(i):
+        pl.semaphore_signal(
+            barrier,
+            inc=1,
+            device_id={"dp": (me + 1 + i) % devices},
+            device_id_type=pl.DeviceIdType.MESH,
+        )
+
+    every(devices - 1, greet)
+
+    def narrow(d):
+        s_out[d] = st_ref[pl.ds(pl.multiple_of(d * 16, 16), 16), :].astype(jnp.bfloat16)
+
+    every(devices, narrow)
+    pl.semaphore_wait(barrier, devices - 1)
+
+    def send_near(k):
+        every(quads - 1, lambda i: near(k, (quad + 1 + i) % quads).start())
+
+    send_near(0)
+    every(devices - 1, lambda i: init_copy((me + 1 + i) % devices).start())
+    send_near(1)
+    mine = pl.ds(pl.multiple_of(me * tokens, tokens), tokens)
+    b_buf[mine, :] = bc_ref[quad, :, :width]
+    c_buf[mine, :] = bc_ref[quad, :, width:]
+    s_in[me] = s_out[me]
+
+    wide = dt_ref[...].astype(jnp.float32)
+    for j in range(blocks):
+        rows_scr[2 * j : 2 * j + 2, :] = wide[:, j * L : (j + 1) * L]
+    row = lax.broadcasted_iota(jnp.int32, (2 * blocks, L), 0)
+    lane = lax.broadcasted_iota(jnp.int32, (2 * blocks, L), 1)
+    first_head = row % 2 == 0
+    raw = rows_scr[0 : 2 * blocks, :] + jnp.where(first_head, bias_ref[0], bias_ref[1])
+    step = jnp.maximum(raw, 0.0) + jnp.log1p(jnp.exp(-jnp.abs(raw)))
+    cum = -step * jnp.where(first_head, rate_ref[0], rate_ref[1])
+    shift = 1
+    while shift < L:
+        cum = cum + jnp.where(lane >= shift, pltpu.roll(cum, shift, 1), 0.0)
+        shift *= 2
+    total = cum[:, L - 1 : L]
+    tail = step * jnp.exp(total - cum)
+    growth = jnp.exp(cum)
+    rows_scr[0 : 2 * blocks, :] = cum
+    rows_scr[2 * blocks : 4 * blocks, :] = step
+    edge_scr[...] = jnp.broadcast_to(jnp.exp(total), (2 * blocks, L))
+    stacked = jnp.concatenate([cum, tail, growth, step], axis=0)
+    cols_scr[...] = jnp.transpose(stacked)
+
+    square_row = lax.broadcasted_iota(jnp.int32, (L, L), 0)
+    square_lane = lax.broadcasted_iota(jnp.int32, (L, L), 1)
+    causal = square_row >= square_lane
+    half = square_lane < L // 2
+    gap = 2 * blocks
+
+    def rows_of(j):
+        return pl.ds(pl.multiple_of(j * L, L), L)
+
+    def prepare(j):
+        turned = pltpu.roll(cols_scr[...], (L - 2 * j) % L, 1)
+
+        def spread(at):
+            return jnp.where(half, turned[:, at : at + 1], turned[:, at + 1 : at + 2])
+
+        carried[rows_of(j), :] = (
+            x_ref[rows_of(j), :].astype(jnp.float32) * spread(gap)
+        ).astype(jnp.bfloat16)
+        grow[j] = spread(2 * gap)
+        for h in range(2):
+            cum_row = rows_scr[pl.ds(2 * j + h, 1), :]
+            step_row = rows_scr[pl.ds(gap + 2 * j + h, 1), :]
+            log_gap = turned[:, h : h + 1] - cum_row
+            pair[2 * j + h] = jnp.exp(jnp.where(causal, log_gap, -jnp.inf)) * step_row
+
+    every(blocks, prepare)
+
+    def gather(k, work):
+        def turn(i):
+            @pl.when(i < quads)
+            def _():
+                q = (quad - i + quads) % quads
+
+                @pl.when(i > 0)
+                def _():
+                    near_in(k, q).wait_recv()
+
+                to_side(k, q, spot).start()
+                to_twin(k, q, spot).start()
+
+            @pl.when((i >= 1) & (i < quads + 1))
+            def _():
+                q = (quad - i + 1 + quads) % quads
+                to_side(k, q, side_spot).wait_recv()
+                to_twin_last(k, q, side_spot).start()
+
+            @pl.when(i >= 2)
+            def _():
+                q = (quad - i + 2 + quads) % quads
+                to_twin(k, q, twin_spot).wait_recv()
+                to_twin_last(k, q, diag_spot).wait_recv()
+                work(2 * q)
+                work(2 * q + 1)
+
+        every(quads + 2, turn)
+
+    def add_block(j):
+        added[j] = rows_dot(carried[rows_of(j), :], b_buf[rows_of(j), :])
+
+    gather(0, add_block)
+
+    every(devices - 1, lambda i: init_from((me + 1 + i) % devices).wait_recv())
+    for k in range(owners):
+        for q in range(8):
+            piece = s_in[8 * k + q].astype(jnp.float32)
+            seeds[k, 8 * q : 8 * q + 8, :] = piece[0:8]
+            seeds[k, 64 + 8 * q : 72 + 8 * q, :] = piece[8:16]
+
+    first = [
+        sum(
+            jnp.where(ps_ref[d] < ps_ref[c], tb_ref[d], 0) for d in range(owners)
+        )
+        for c in range(owners)
+    ]
+    end = [first[c] + tb_ref[c] for c in range(owners)]
+    state_row = lax.broadcasted_iota(jnp.int32, (L, width), 0)
+
+    def advance(j, state):
+        is_start = sum(jnp.where(first[c] == j, 1, 0) for c in range(owners))
+        owner = sum(
+            jnp.where((first[c] <= j) & (j < end[c]), om_ref[c], 0) for c in range(owners)
+        )
+        owner = jnp.clip(owner, 0, owners - 1)
+        start = jnp.where(is_start > 0, seeds[owner], state)
+        starts[j] = start.astype(jnp.bfloat16)
+        decay = jnp.where(
+            state_row < L // 2,
+            edge_scr[pl.ds(2 * j, 1), 0:1],
+            edge_scr[pl.ds(2 * j + 1, 1), 0:1],
+        )
+        after = decay * start + added[j]
+        added[j] = after
+        return after
+
+    lax.fori_loop(0, blocks, advance, jnp.zeros((L, width), jnp.float32))
+
+    for k in range(owners):
+        last = sum(jnp.where(om_ref[c] == k, end[c] - 1, 0) for c in range(owners))
+        done = added[jnp.clip(last, 0, blocks - 1)]
+        for q in range(8):
+            f_out[8 * k + q] = jnp.concatenate(
+                [done[8 * q : 8 * q + 8], done[64 + 8 * q : 72 + 8 * q]], axis=0
+            ).astype(jnp.bfloat16)
+    every(devices - 1, lambda i: fin_copy((me + 1 + i) % devices).start())
+    f_in[me] = f_out[me]
+
+    skip_lane = jnp.where(square_lane[0:1] < L // 2, skip_ref[0], skip_ref[1])
+    cols_scr[...] = jnp.zeros((L, L), jnp.float32)
+
+    def out_block(j):
+        rows = rows_of(j)
+        c_block = c_buf[rows, :]
+        x_block = x_ref[rows, :]
+        scores = lanes_dot(c_block, b_buf[rows, :])
+        parts = [
+            jnp.dot(
+                (scores * pair[2 * j + h]).astype(jnp.bfloat16),
+                x_block,
+                preferred_element_type=jnp.float32,
+            )
+            for h in range(2)
+        ]
+        from_state = grow[j] * lanes_dot(c_block, starts[j])
+        mixed = (
+            jnp.where(half, parts[0], parts[1])
+            + from_state
+            + skip_lane * x_block.astype(jnp.float32)
+        )
+        z_block = z_ref[rows, :].astype(jnp.float32)
+        result = mixed * (z_block / (1.0 + jnp.exp(-z_block)))
+        gated[rows, :] = result
+        total_square = jnp.sum(result * result, axis=1, keepdims=True)
+        cols_scr[...] = jnp.where(square_lane == j, total_square, cols_scr[...])
+
+    gather(1, out_block)
+
+    sq_out[...] = jnp.transpose(cols_scr[...])[0:blocks]
+
+    def sq_copy(i):
+        other = (spot + 1 + i) % 4
+        return remote(sq_out, sq_in.at[spot], sq_send.at[other], sq_recv.at[spot], 4 * quad + other)
+
+    def sq_from(i):
+        other = (spot + 1 + i) % 4
+        return remote(sq_out, sq_in.at[other], sq_send.at[other], sq_recv.at[other], side)
+
+    every(3, lambda i: sq_copy(i).start())
+    sq_in[spot] = sq_out[...]
+    every(devices - 1, lambda i: fin_from((me + 1 + i) % devices).wait_recv())
+
+    def widen(d):
+        ns_ref[pl.ds(pl.multiple_of(d * 16, 16), 16), :] = f_in[d].astype(jnp.float32)
+
+    every(devices, widen)
+    every(3, lambda i: sq_from(i).wait_recv())
+    group_square = (sq_in[0] + sq_in[1]) + (sq_in[2] + sq_in[3])
+    inverse = lax.rsqrt(group_square / (4 * L) + 1e-05)
+    cols_scr[...] = jnp.transpose(
+        jnp.concatenate([inverse, jnp.zeros((L - blocks, L), jnp.float32)], axis=0)
+    )
+    gain = gain_ref[...]
+
+    def norm_block(j):
+        turned = pltpu.roll(cols_scr[...], (L - j) % L, 1)
+        y_ref[rows_of(j), :] = (gated[rows_of(j), :] * turned[:, 0:1] * gain).astype(jnp.bfloat16)
+
+    every(blocks, norm_block)
+
+    def drain(q):
+        for k in range(2):
+
+            @pl.when(q != quad)
+            def _():
+                near(k, q).wait_send()
+
+            to_side(k, q, spot).wait_send()
+            to_twin(k, q, spot).wait_send()
+            to_twin_last(k, q, side_spot).wait_send()
+
+    every(quads, drain)
+
+    def drain_states(i):
+        d = (me + 1 + i) % devices
+        init_copy(d).wait_send()
+        fin_copy(d).wait_send()
+
+    every(devices - 1, drain_states)
+    every(3, lambda i: sq_copy(i).wait_send())
+
+
+def fused(
+    x_in,
+    z_in,
+    dt_in,
+    bc_in,
+    owner_states,
+    decay_rate,
+    dt_bias,
+    skip_d,
+    norm_gain,
+    owner_map,
+    prefill_slot,
+    turn_blocks,
+):
+    devices = lax.axis_size("dp")
+    tokens, columns = x_in.shape
+    blocks = tokens // BLOCK_LEN
+    owners = owner_map.shape[0]
+    state = bc_in.shape[2] // 2
+    quads = devices // 4
+    vmem = pl.BlockSpec(memory_space=pltpu.VMEM)
+    smem = pl.BlockSpec(memory_space=pltpu.SMEM)
+    f32, bf16 = jnp.float32, jnp.bfloat16
+    L = BLOCK_LEN
+    dma = pltpu.SemaphoreType.DMA
+    y_out, new_states = pl.pallas_call(
+        functools.partial(layer_kernel, devices, blocks, owners),
+        out_shape=(
+            jax.ShapeDtypeStruct((tokens, columns), bf16),
+            jax.ShapeDtypeStruct((devices * 16, state), f32),
+        ),
+        in_specs=[smem] * 6 + [vmem] * 6,
+        out_specs=(vmem, vmem),
+        scratch_shapes=[
+            pltpu.VMEM((tokens, state), bf16),
+            pltpu.VMEM((tokens, state), bf16),
+            pltpu.VMEM((devices, 16, state), bf16),
+            pltpu.VMEM((devices, 16, state), bf16),
+            pltpu.VMEM((devices, 16, state), bf16),
+            pltpu.VMEM((devices, 16, state), bf16),
+            pltpu.VMEM((blocks, L), f32),
+            pltpu.VMEM((4, blocks, L), f32),
+            pltpu.VMEM((owners, L, state), f32),
+            pltpu.VMEM((2 * blocks, L, L), f32),
+            pltpu.VMEM((blocks, L, L), f32),
+            pltpu.VMEM((blocks, L, state), f32),
+            pltpu.VMEM((blocks, L, state), bf16),
+            pltpu.VMEM((tokens, columns), bf16),
+            pltpu.VMEM((tokens, columns), f32),
+            pltpu.VMEM((4 * blocks, L), f32),
+            pltpu.VMEM((L, L), f32),
+            pltpu.VMEM((2 * blocks, L), f32),
+        ]
+        + [dma((2, quads))] * 8
+        + [dma((devices,))] * 4
+        + [dma((4,))] * 2,
+        compiler_params=pltpu.CompilerParams(
+            collective_id=0, has_side_effects=True, vmem_limit_bytes=40 * 1024 * 1024
+        ),
+    )(
+        owner_map,
+        prefill_slot,
+        turn_blocks,
+        dt_bias,
+        decay_rate,
+        skip_d,
+        x_in,
+        z_in,
+        dt_in,
+        bc_in,
+        owner_states.reshape(-1, state),
+        norm_gain.reshape(1, columns),
+    )
+    return (y_out, new_states.reshape(owner_states.shape))
+
+
+def choose(*arrays):
+    x_in, dt_in, bc_in, owner_states, owner_map = (arrays[i] for i in (0, 2, 3, 4, 9))
+    devices = lax.axis_size("dp")
+    fits = (
+        devices == 4 * bc_in.shape[0]
+        and x_in.shape[0] == 16 * BLOCK_LEN
+        and x_in.shape[1] == BLOCK_LEN
+        and dt_in.shape[0] == 2
+        and owner_states.shape[1] == 1
+        and owner_states.shape[3] == 8
+        and devices == 8 * owner_map.shape[0]
+    )
+    return (fused if fits else shards)(*arrays)
+
+
 def solution(mesh):
     placed = (
         P("groups", "dp"),
@@ -160,7 +619,7 @@
         P("groups"),
     )
     return jax.shard_map(
-        shards,
+        choose,
         mesh=mesh,
         in_specs=placed,
         out_specs=(P("groups", "dp"), P(("groups", "dp"), None, None, None, None)),

time: 109 us -> 63 us (0.58)
  Pallas kernels: 0 us -> 54.8 us
  waiting for transfers between devices: 42.3 us -> 0 us
  blocking collectives: 17.7 us -> 0 us
  local copies, waits for them, and re-layouts: 22.5 us -> 7.14 us
  matrix products: 9.77 us -> 0 us
  starting transfers between devices: 9.41 us -> 0 us
  other arithmetic: 5.59 us -> 0 us
    pallas_call x0 -> x1, Pallas kernels: none -> 54.8 us  [fused(): pl.pallas_call(functools.partial(layer_kernel, devices, blocks, owners),...]
    all_to_all x2 -> x0, waiting for transfers between devices: 39.8 us -> none  [the longest x1 35.7 us: shards(): lax.all_to_all(copies, 'dp', split_axis=0, concat_axis=1, tiled=True)[0]]
    all_to_all x1 -> x0, blocking collectives: 17.7 us -> none  [fetch_states(): lax.all_to_all(owner_states[0].astype(jnp.bfloat16), 'dp', split_axis=1,...]
    dot_general x5 -> x0, matrix products: 9.77 us -> none  [the longest x1 5.38 us: shards(): jnp.einsum('hrj,jhps->rhps', carry_weight, block_input, precision=exact_m...]
    all_to_all x2 -> x0, starting transfers between devices: 7.67 us -> none  [the longest x1 4.05 us: shards(): lax.all_to_all(outgoing, 'dp', split_axis=2, concat_axis=1, tiled=True)]
    slice x6 -> x0, local copies, waits for them, and re-layouts: 3.69 us -> none  [the longest x1 2.72 us: shards(): bc_group[:, :state_width].reshape(block_count, BLOCK_LEN, state_width)]
    reshape x3 -> x0, local copies, waits for them, and re-layouts: 3.38 us -> none  [the longest x2 2.18 us: shards(): value_blocks = x_in.reshape(block_count, BLOCK_LEN, head_local, head_width)]
    convert_element_type x3 -> x0, local copies, waits for them, and re-layouts: 3.28 us -> none  [the longest x2 3.24 us: shards(): gated = mixer_out * jax.nn.silu(gate_blocks.astype(jnp.float32))]
  transfers between devices with their start and end apart: 4 -> 0, of which waited for: 4 -> 0; matrix products, arithmetic and copies ran while one was open for 18% -> 0% of each run, Pallas kernels for 0% -> 0%
where the time goes in v1:
time: 63 us; the launch traced here: 62.7 us
  Pallas kernels  54.8 us (87%)
  local copies, waits for them, and re-layouts  7.14 us (11%)
  between operations  0.71 us (1%)
    pallas_call x1, Pallas kernels, fused(): pl.pallas_call(functools.partial(layer_kernel, devices, blocks, owners),...  54.8 us
    unnamed x26, local copies, waits for them, and re-layouts  7.14 us

profile of v1, /device:TPU:0, one launch (start us, length us, event | category | flops | bytes accessed | tf_op | source)
XLA Modules:
  0.0 62.7 jit_solution(5773840129883376815)
XLA Ops:
  0.6 0.0 copy-start.8
  0.6 0.0 copy-start.9
  0.7 0.0 copy-start.10
  0.7 0.0 copy-start.11
  0.7 0.0 copy-start.5
  0.7 0.0 copy-start.6
  0.7 0.0 copy-start.7
  0.7 0.6 copy-done.8
  1.3 0.0 copy-done.9
  1.3 0.0 copy-done.10
  1.3 0.0 copy-done.11
  1.3 0.0 copy-done.5
  1.4 0.0 copy-done.6
  1.4 0.0 copy-done.7
  1.4 0.0 copy-start
  1.4 1.0 %copy-done = bf16[2048,128]{1,0:T(8,128)(2,1)S(1)} copy-done((bf16[2048,128]{1,0:T(8,128)(2,1)S(1)}, bf16[2048,128]{1,0:T(8,128)(2,1)}, u32[]{:S(2)}) %copy-start) | copy-done | bytes 524312
  2.4 0.0 copy-start.1
  2.4 1.0 %copy-done.1 = bf16[2048,128]{1,0:T(8,128)(2,1)S(1)} copy-done((bf16[2048,128]{1,0:T(8,128)(2,1)S(1)}, bf16[2048,128]{1,0:T(8,128)(2,1)}, u32[]{:S(2)}) %copy-start.1) | copy-done | bytes 524312
  3.5 0.0 copy-start.2
  3.5 1.0 %copy-done.2 = bf16[8,64,512]{2,1,0:T(8,128)(2,1)S(1)} copy-done((bf16[8,64,512]{2,1,0:T(8,128)(2,1)S(1)}, bf16[8,64,512]{2,1,0:T(8,128)(2,1)}, u32[]{:S(2)}) %copy-start.2) | copy-done | bytes 524312
  4.5 0.0 copy-start.3
  4.5 1.0 %copy-done.3 = f32[1,1,64,8,256]{4,3,2,1,0:T(8,128)S(1)} copy-done((f32[1,1,64,8,256]{4,3,2,1,0:T(8,128)S(1)}, f32[1,1,64,8,256]{4,3,2,1,0:T(8,128)}, u32[]{:S(2)}) %copy-start.3) | copy-done | bytes 524312
  5.6 0.0 copy-start.4
  5.6 0.7 %copy-done.4 = bf16[2,2048]{1,0:T(2,128)(2,1)S(1)} copy-done((bf16[2,2048]{1,0:T(2,128)(2,1)S(1)}, bf16[2,2048]{1,0:T(2,128)(2,1)}, u32[]{:S(2)}) %copy-start.4) | copy-done | bytes 8216
  6.3 54.8 %shard_map.131 = (bf16[2048,128]{1,0:T(8,128)(2,1)S(1)}, f32[512,256]{1,0:T(8,128)S(1)}) custom-call(s32[4]{0:T(128)S(1)} %copy-done.5, s32[4]{0:T(128)S(1)} %copy-done.6, s32[4]{0:T(128)S(1)} %copy-done.7, f32[2]{0:T(128)S(1)} %copy-done.8, f32[2]{0:T(128)S(1)} %copy-done.9, f32[2]{0:T(128)S(1)} %copy-done.10, bf16[2048,128]{1,0:T(8,128)(2,1)S(1)} %copy-done, ...), custom_call_target="tpu_custom_call" | custom-call | tf_op jit(solution)/shard_map/pallas_call | solution.py:540
  61.1 0.8 %copy.16 = bf16[2048,128]{1,0:T(8,128)(2,1)} copy(bf16[2048,128]{1,0:T(8,128)(2,1)S(1)} %get-tuple-element.8) | data formatting | bytes 1048576
  61.9 0.8 %copy.17 = f32[1,1,64,8,256]{4,3,2,1,0:T(8,128)} copy(f32[1,1,64,8,256]{4,3,2,1,0:T(8,128)S(1)} %bitcast.4) | data formatting | bytes 1048576
Async XLA Ops:
  0.6 0.7 %copy-start.8 = (f32[2]{0:T(128)S(1)}, f32[2]{0:T(128)}, u32[]{:S(2)}) copy-start(f32[2]{0:T(128)} %bias_ref.1) | copy-start | bytes 28
  0.6 0.7 %copy-start.9 = (f32[2]{0:T(128)S(1)}, f32[2]{0:T(128)}, u32[]{:S(2)}) copy-start(f32[2]{0:T(128)} %rate_ref.1) | copy-start | bytes 28
  0.7 0.7 %copy-start.10 = (f32[2]{0:T(128)S(1)}, f32[2]{0:T(128)}, u32[]{:S(2)}) copy-start(f32[2]{0:T(128)} %skip_ref.1) | copy-start | bytes 28
  0.7 0.7 %copy-start.11 = (f32[128]{0:T(128)S(1)}, f32[128]{0:T(128)}, u32[]{:S(2)}) copy-start(f32[128]{0:T(128)} %param.20) | copy-start | bytes 1540
  0.7 0.7 %copy-start.5 = (s32[4]{0:T(128)S(1)}, s32[4]{0:T(128)}, u32[]{:S(2)}) copy-start(s32[4]{0:T(128)} %om_ref.1) | copy-start | bytes 52
  0.7 0.7 %copy-start.6 = (s32[4]{0:T(128)S(1)}, s32[4]{0:T(128)}, u32[]{:S(2)}) copy-start(s32[4]{0:T(128)} %ps_ref.1) | copy-start | bytes 52
  0.7 0.7 %copy-start.7 = (s32[4]{0:T(128)S(1)}, s32[4]{0:T(128)}, u32[]{:S(2)}) copy-start(s32[4]{0:T(128)} %tb_ref.1) | copy-start | bytes 52
  1.4 1.0 %copy-start = (bf16[2048,128]{1,0:T(8,128)(2,1)S(1)}, bf16[2048,128]{1,0:T(8,128)(2,1)}, u32[]{:S(2)}) copy-start(bf16[2048,128]{1,0:T(8,128)(2,1)} %x_ref.1) | copy-start | bytes 1572868
  2.4 1.0 %copy-start.1 = (bf16[2048,128]{1,0:T(8,128)(2,1)S(1)}, bf16[2048,128]{1,0:T(8,128)(2,1)}, u32[]{:S(2)}) copy-start(bf16[2048,128]{1,0:T(8,128)(2,1)} %z_ref.1) | copy-start | bytes 1572868
  3.5 1.0 %copy-start.2 = (bf16[8,64,512]{2,1,0:T(8,128)(2,1)S(1)}, bf16[8,64,512]{2,1,0:T(8,128)(2,1)}, u32[]{:S(2)}) copy-start(bf16[8,64,512]{2,1,0:T(8,128)(2,1)} %bc_ref.1) | copy-start | bytes 1572868
  4.5 1.0 %copy-start.3 = (f32[1,1,64,8,256]{4,3,2,1,0:T(8,128)S(1)}, f32[1,1,64,8,256]{4,3,2,1,0:T(8,128)}, u32[]{:S(2)}) copy-start(f32[1,1,64,8,256]{4,3,2,1,0:T(8,128)} %param.16) | copy-start | bytes 1572868
  5.6 0.7 %copy-start.4 = (bf16[2,2048]{1,0:T(2,128)(2,1)S(1)}, bf16[2,2048]{1,0:T(2,128)(2,1)}, u32[]{:S(2)}) copy-start(bf16[2,2048]{1,0:T(2,128)(2,1)} %dt_ref.1) | copy-start | bytes 24580

commit v2 on v1

--- a/solution.py
+++ b/solution.py
@@ -166,14 +166,17 @@
     bias_ref,
     rate_ref,
     skip_ref,
+    dt_ref,
+    gain_ref,
+    x_hbm,
+    z_hbm,
+    bc_ref,
+    st_hbm,
+    y_ref,
+    ns_ref,
     x_ref,
     z_ref,
-    dt_ref,
-    bc_ref,
     st_ref,
-    gain_ref,
-    y_ref,
-    ns_ref,
     b_buf,
     c_buf,
     s_out,
@@ -206,6 +209,7 @@
     fin_recv,
     sq_send,
     sq_recv,
+    load_sem,
 ):
     me = lax.axis_index("dp")
     L = BLOCK_LEN
@@ -271,6 +275,21 @@
     def every(count, body):
         lax.fori_loop(0, count, lambda i, c: (body(i), c)[1], 0)
 
+    mine = pl.ds(pl.multiple_of(me * tokens, tokens), tokens)
+    loads = [
+        pltpu.make_async_copy(src, dst, load_sem.at[i])
+        for i, (src, dst) in enumerate(
+            (
+                (st_hbm, st_ref),
+                (x_hbm, x_ref),
+                (bc_ref.at[quad, :, 0:width], b_buf.at[mine, :]),
+                (bc_ref.at[quad, :, width : 2 * width], c_buf.at[mine, :]),
+                (z_hbm, z_ref),
+            )
+        )
+    ]
+    for load in loads:
+        load.start()
     barrier = pltpu.get_barrier_semaphore()
 
     def greet(i):
@@ -286,6 +305,7 @@
     def narrow(d):
         s_out[d] = st_ref[pl.ds(pl.multiple_of(d * 16, 16), 16), :].astype(jnp.bfloat16)
 
+    loads[0].wait()
     every(devices, narrow)
     pl.semaphore_wait(barrier, devices - 1)
 
@@ -295,9 +315,6 @@
     send_near(0)
     every(devices - 1, lambda i: init_copy((me + 1 + i) % devices).start())
     send_near(1)
-    mine = pl.ds(pl.multiple_of(me * tokens, tokens), tokens)
-    b_buf[mine, :] = bc_ref[quad, :, :width]
-    c_buf[mine, :] = bc_ref[quad, :, width:]
     s_in[me] = s_out[me]
 
     wide = dt_ref[...].astype(jnp.float32)
@@ -347,7 +364,11 @@
             log_gap = turned[:, h : h + 1] - cum_row
             pair[2 * j + h] = jnp.exp(jnp.where(causal, log_gap, -jnp.inf)) * step_row
 
+    loads[1].wait()
     every(blocks, prepare)
+    loads[2].wait()
+    loads[3].wait()
+    loads[4].wait()
 
     def gather(k, work):
         def turn(i):
@@ -543,9 +564,12 @@
             jax.ShapeDtypeStruct((tokens, columns), bf16),
             jax.ShapeDtypeStruct((devices * 16, state), f32),
         ),
-        in_specs=[smem] * 6 + [vmem] * 6,
+        in_specs=[smem] * 6 + [vmem] * 2 + [pl.BlockSpec(memory_space=pl.ANY)] * 4,
         out_specs=(vmem, vmem),
         scratch_shapes=[
+            pltpu.VMEM((tokens, columns), bf16),
+            pltpu.VMEM((tokens, columns), bf16),
+            pltpu.VMEM((devices * 16, state), f32),
             pltpu.VMEM((tokens, state), bf16),
             pltpu.VMEM((tokens, state), bf16),
             pltpu.VMEM((devices, 16, state), bf16),
@@ -567,7 +591,8 @@
         ]
         + [dma((2, quads))] * 8
         + [dma((devices,))] * 4
-        + [dma((4,))] * 2,
+        + [dma((4,))] * 2
+        + [dma((5,))],
         compiler_params=pltpu.CompilerParams(
             collective_id=0, has_side_effects=True, vmem_limit_bytes=40 * 1024 * 1024
         ),
@@ -578,12 +603,12 @@
         dt_bias,
         decay_rate,
         skip_d,
+        dt_in,
+        norm_gain.reshape(1, columns),
         x_in,
         z_in,
-        dt_in,
         bc_in,
         owner_states.reshape(-1, state),
-        norm_gain.reshape(1, columns),
     )
     return (y_out, new_states.reshape(owner_states.shape))
 

time: 63 us -> 63.2 us (level)
  no operation moved by 1% of the time
where the time goes in v2:
time: 63.2 us; the launch traced here: 62.9 us
  Pallas kernels  55 us (87%)
  local copies, waits for them, and re-layouts  7.14 us (11%)
  between operations  0.71 us (1%)
    pallas_call x1, Pallas kernels, fused(): pl.pallas_call(functools.partial(layer_kernel, devices, blocks, owners),...  55 us
    unnamed x26, local copies, waits for them, and re-layouts  7.14 us

profile of v2, /device:TPU:0, one launch (start us, length us, event | category | flops | bytes accessed | tf_op | source)
XLA Modules:
  0.0 62.9 jit_solution(1307570358103573516)
XLA Ops:
  0.6 0.0 copy-start.8
  0.6 0.0 copy-start.9
  0.7 0.0 copy-start.10
  0.7 0.0 copy-start.11
  0.7 0.0 copy-start.5
  0.7 0.0 copy-start.6
  0.7 0.0 copy-start.7
  0.7 0.6 copy-done.8
  1.3 0.0 copy-done.9
  1.3 0.0 copy-done.10
  1.3 0.0 copy-done.11
  1.3 0.0 copy-done.5
  1.4 0.0 copy-done.6
  1.4 0.0 copy-done.7
  1.4 0.0 copy-start
  1.4 1.0 %copy-done = bf16[2048,128]{1,0:T(8,128)(2,1)S(1)} copy-done((bf16[2048,128]{1,0:T(8,128)(2,1)S(1)}, bf16[2048,128]{1,0:T(8,128)(2,1)}, u32[]{:S(2)}) %copy-start) | copy-done | bytes 524312
  2.4 0.0 copy-start.1
  2.4 1.0 %copy-done.1 = bf16[2048,128]{1,0:T(8,128)(2,1)S(1)} copy-done((bf16[2048,128]{1,0:T(8,128)(2,1)S(1)}, bf16[2048,128]{1,0:T(8,128)(2,1)}, u32[]{:S(2)}) %copy-start.1) | copy-done | bytes 524312
  3.5 0.0 copy-start.2
  3.5 1.0 %copy-done.2 = bf16[8,64,512]{2,1,0:T(8,128)(2,1)S(1)} copy-done((bf16[8,64,512]{2,1,0:T(8,128)(2,1)S(1)}, bf16[8,64,512]{2,1,0:T(8,128)(2,1)}, u32[]{:S(2)}) %copy-start.2) | copy-done | bytes 524312
  4.5 0.0 copy-start.3
  4.5 1.0 %copy-done.3 = f32[1,1,64,8,256]{4,3,2,1,0:T(8,128)S(1)} copy-done((f32[1,1,64,8,256]{4,3,2,1,0:T(8,128)S(1)}, f32[1,1,64,8,256]{4,3,2,1,0:T(8,128)}, u32[]{:S(2)}) %copy-start.3) | copy-done | bytes 524312
  5.6 0.0 copy-start.4
  5.6 0.7 %copy-done.4 = bf16[2,2048]{1,0:T(2,128)(2,1)S(1)} copy-done((bf16[2,2048]{1,0:T(2,128)(2,1)S(1)}, bf16[2,2048]{1,0:T(2,128)(2,1)}, u32[]{:S(2)}) %copy-start.4) | copy-done | bytes 8216
  6.3 55.0 %shard_map.131 = (bf16[2048,128]{1,0:T(8,128)(2,1)S(1)}, f32[512,256]{1,0:T(8,128)S(1)}) custom-call(s32[4]{0:T(128)S(1)} %copy-done.5, s32[4]{0:T(128)S(1)} %copy-done.6, s32[4]{0:T(128)S(1)} %copy-done.7, f32[2]{0:T(128)S(1)} %copy-done.8, f32[2]{0:T(128)S(1)} %copy-done.9, f32[2]{0:T(128)S(1)} %copy-done.10, bf16[2,2048]{1,0:T(2,128)(2,1)S(1)} %copy-done.4, ...), custom_call_target="tpu_custom_call" | custom-call | tf_op jit(solution)/shard_map/pallas_call | solution.py:561
  61.3 0.8 %copy.16 = bf16[2048,128]{1,0:T(8,128)(2,1)} copy(bf16[2048,128]{1,0:T(8,128)(2,1)S(1)} %get-tuple-element.8) | data formatting | bytes 1048576
  62.1 0.8 %copy.17 = f32[1,1,64,8,256]{4,3,2,1,0:T(8,128)} copy(f32[1,1,64,8,256]{4,3,2,1,0:T(8,128)S(1)} %bitcast.4) | data formatting | bytes 1048576
Async XLA Ops:
  0.6 0.7 %copy-start.8 = (f32[2]{0:T(128)S(1)}, f32[2]{0:T(128)}, u32[]{:S(2)}) copy-start(f32[2]{0:T(128)} %bias_ref.1) | copy-start | bytes 28
  0.6 0.7 %copy-start.9 = (f32[2]{0:T(128)S(1)}, f32[2]{0:T(128)}, u32[]{:S(2)}) copy-start(f32[2]{0:T(128)} %rate_ref.1) | copy-start | bytes 28
  0.7 0.7 %copy-start.10 = (f32[2]{0:T(128)S(1)}, f32[2]{0:T(128)}, u32[]{:S(2)}) copy-start(f32[2]{0:T(128)} %skip_ref.1) | copy-start | bytes 28
  0.7 0.7 %copy-start.11 = (f32[128]{0:T(128)S(1)}, f32[128]{0:T(128)}, u32[]{:S(2)}) copy-start(f32[128]{0:T(128)} %param.20) | copy-start | bytes 1540
  0.7 0.7 %copy-start.5 = (s32[4]{0:T(128)S(1)}, s32[4]{0:T(128)}, u32[]{:S(2)}) copy-start(s32[4]{0:T(128)} %om_ref.1) | copy-start | bytes 52
  0.7 0.7 %copy-start.6 = (s32[4]{0:T(128)S(1)}, s32[4]{0:T(128)}, u32[]{:S(2)}) copy-start(s32[4]{0:T(128)} %ps_ref.1) | copy-start | bytes 52
  0.7 0.7 %copy-start.7 = (s32[4]{0:T(128)S(1)}, s32[4]{0:T(128)}, u32[]{:S(2)}) copy-start(s32[4]{0:T(128)} %tb_ref.1) | copy-start | bytes 52
  1.4 1.0 %copy-start = (bf16[2048,128]{1,0:T(8,128)(2,1)S(1)}, bf16[2048,128]{1,0:T(8,128)(2,1)}, u32[]{:S(2)}) copy-start(bf16[2048,128]{1,0:T(8,128)(2,1)} %x_hbm.1) | copy-start | bytes 1572868
  2.4 1.0 %copy-start.1 = (bf16[2048,128]{1,0:T(8,128)(2,1)S(1)}, bf16[2048,128]{1,0:T(8,128)(2,1)}, u32[]{:S(2)}) copy-start(bf16[2048,128]{1,0:T(8,128)(2,1)} %z_hbm.1) | copy-start | bytes 1572868
  3.5 1.0 %copy-start.2 = (bf16[8,64,512]{2,1,0:T(8,128)(2,1)S(1)}, bf16[8,64,512]{2,1,0:T(8,128)(2,1)}, u32[]{:S(2)}) copy-start(bf16[8,64,512]{2,1,0:T(8,128)(2,1)} %bc_ref.1) | copy-start | bytes 1572868
  4.5 1.0 %copy-start.3 = (f32[1,1,64,8,256]{4,3,2,1,0:T(8,128)S(1)}, f32[1,1,64,8,256]{4,3,2,1,0:T(8,128)}, u32[]{:S(2)}) copy-start(f32[1,1,64,8,256]{4,3,2,1,0:T(8,128)} %param.16) | copy-start | bytes 1572868
  5.6 0.7 %copy-start.4 = (bf16[2,2048]{1,0:T(2,128)(2,1)S(1)}, bf16[2,2048]{1,0:T(2,128)(2,1)}, u32[]{:S(2)}) copy-start(bf16[2,2048]{1,0:T(2,128)(2,1)} %dt_ref.1) | copy-start | bytes 24580

commit v3 on v2

--- a/solution.py
+++ b/solution.py
@@ -224,6 +224,14 @@
     bufs = (b_buf, c_buf)
     tokens = bc_ref.shape[1]
 
+    depth_at = quad // 2
+    codes = (0 + 4 * 1 + 16 * 2 + 64 * 3, 1 + 4 * 2 + 16 * 0 + 64 * 3, 2 + 4 * 1 + 16 * 3 + 64 * 0, 3 + 4 * 2 + 16 * 1 + 64 * 0)
+    code = sum(jnp.where(depth_at == d, codes[d], 0) for d in range(4))
+
+    def nth(i):
+        scale = sum(jnp.where(i // 2 == d, 4**d, 0) for d in range(4))
+        return 2 * ((code // scale) % 4) + (quad + i) % 2
+
     def remote(src, dst, send, recv, to):
         return pltpu.make_async_remote_copy(
             src_ref=src,
@@ -309,12 +317,8 @@
     every(devices, narrow)
     pl.semaphore_wait(barrier, devices - 1)
 
-    def send_near(k):
-        every(quads - 1, lambda i: near(k, (quad + 1 + i) % quads).start())
-
-    send_near(0)
+    every(quads - 1, lambda i: near(0, nth(i + 1)).start())
     every(devices - 1, lambda i: init_copy((me + 1 + i) % devices).start())
-    send_near(1)
     s_in[me] = s_out[me]
 
     wide = dt_ref[...].astype(jnp.float32)
@@ -374,7 +378,7 @@
         def turn(i):
             @pl.when(i < quads)
             def _():
-                q = (quad - i + quads) % quads
+                q = nth(i)
 
                 @pl.when(i > 0)
                 def _():
@@ -382,16 +386,21 @@
 
                 to_side(k, q, spot).start()
                 to_twin(k, q, spot).start()
+                if k == 0:
+
+                    @pl.when(i > 0)
+                    def _():
+                        near(1, q).start()
 
             @pl.when((i >= 1) & (i < quads + 1))
             def _():
-                q = (quad - i + 1 + quads) % quads
+                q = nth(i - 1)
                 to_side(k, q, side_spot).wait_recv()
                 to_twin_last(k, q, side_spot).start()
 
             @pl.when(i >= 2)
             def _():
-                q = (quad - i + 2 + quads) % quads
+                q = nth(i - 2)
                 to_twin(k, q, twin_spot).wait_recv()
                 to_twin_last(k, q, diag_spot).wait_recv()
                 work(2 * q)
@@ -594,7 +603,7 @@
         + [dma((4,))] * 2
         + [dma((5,))],
         compiler_params=pltpu.CompilerParams(
-            collective_id=0, has_side_effects=True, vmem_limit_bytes=40 * 1024 * 1024
+            collective_id=0, has_side_effects=True, vmem_limit_bytes=63 * 1024 * 1024
         ),
     )(
         owner_map,

time: 63.2 us -> 59.9 us (0.948)
  local copies, waits for them, and re-layouts: 7.14 us -> 2.72 us
  Pallas kernels: 55 us -> 56.3 us
    unnamed x26 -> x4, local copies, waits for them, and re-layouts: 7.14 us -> 2.72 us
    pallas_call x1, Pallas kernels: 55 us -> 56.3 us  [fused(): pl.pallas_call(functools.partial(layer_kernel, devices, blocks, owners),...]
where the time goes in v3:
time: 59.9 us; the launch traced here: 59.7 us
  Pallas kernels  56.3 us (94%)
  local copies, waits for them, and re-layouts  2.72 us (5%)
  between operations  0.65 us (1%)
    pallas_call x1, Pallas kernels, fused(): pl.pallas_call(functools.partial(layer_kernel, devices, blocks, owners),...  56.3 us
    unnamed x4, local copies, waits for them, and re-layouts  2.72 us

profile of v3, /device:TPU:0, one launch (start us, length us, event | category | flops | bytes accessed | tf_op | source)
XLA Modules:
  0.0 59.7 jit_solution(6680449439236250177)
XLA Ops:
  0.6 56.3 %shard_map.131 = (bf16[2048,128]{1,0:T(8,128)(2,1)}, f32[512,256]{1,0:T(8,128)}) custom-call(s32[4]{0:T(128)} %om_ref.1, s32[4]{0:T(128)} %ps_ref.1, s32[4]{0:T(128)} %tb_ref.1, f32[2]{0:T(128)} %bias_ref.1, f32[2]{0:T(128)} %rate_ref.1, f32[2]{0:T(128)} %skip_ref.1, bf16[2,2048]{1,0:T(2,128)(2,1)} %dt_ref.1, f32[1,128]{1,0:T(1,128)} %bitcast.5, ...), custom_call_target="tpu_custom_call" | custom-call | tf_op jit(solution)/shard_map/pallas_call | solution.py:570
  56.9 0.0 copy-start
  56.9 1.9 %copy.16 = bf16[2048,128]{1,0:T(8,128)(2,1)} copy(bf16[2048,128]{1,0:T(8,128)(2,1)} %get-tuple-element.8) | data formatting | bytes 1048576
  58.9 0.0 copy-done
  58.9 0.8 %copy.17 = f32[1,1,64,8,256]{4,3,2,1,0:T(8,128)} copy(f32[1,1,64,8,256]{4,3,2,1,0:T(8,128)S(1)} %bitcast.4) | data formatting | bytes 1048576
Async XLA Ops:
  56.9 1.9 %copy-start = (f32[512,256]{1,0:T(8,128)S(1)}, f32[512,256]{1,0:T(8,128)}, u32[]{:S(2)}) copy-start(f32[512,256]{1,0:T(8,128)} %get-tuple-element.5) | copy-start | bytes 1572868

commit v4 on v3

--- a/solution.py
+++ b/solution.py
@@ -177,8 +177,7 @@
     x_ref,
     z_ref,
     st_ref,
-    b_buf,
-    c_buf,
+    buf,
     s_out,
     s_in,
     f_out,
@@ -195,6 +194,7 @@
     rows_scr,
     cols_scr,
     edge_scr,
+    sums_scr,
     near_send,
     near_recv,
     side_send,
@@ -220,9 +220,9 @@
     side = me + 2 - 4 * ((me // 2) % 2)
     twin_spot, side_spot = twin % 4, side % 4
     diag_spot = 3 - spot
-    width = b_buf.shape[1]
-    bufs = (b_buf, c_buf)
+    width = buf.shape[1]
     tokens = bc_ref.shape[1]
+    rows_each = devices * tokens
 
     depth_at = quad // 2
     codes = (0 + 4 * 1 + 16 * 2 + 64 * 3, 1 + 4 * 2 + 16 * 0 + 64 * 3, 2 + 4 * 1 + 16 * 3 + 64 * 0, 3 + 4 * 2 + 16 * 1 + 64 * 0)
@@ -243,11 +243,11 @@
         )
 
     def chunk(k, q, s):
-        return bufs[k].at[pl.ds(pl.multiple_of((4 * q + s) * tokens, tokens), tokens), :]
+        return buf.at[pl.ds(pl.multiple_of(k * rows_each + (4 * q + s) * tokens, tokens), tokens), :]
 
     def near(k, q):
         return remote(
-            bc_ref.at[q, :, k * width : (k + 1) * width],
+            bc_ref.at[q, :, pl.ds(pl.multiple_of(k * width, width), width)],
             chunk(k, quad, spot),
             near_send.at[k, q],
             near_recv.at[k, quad],
@@ -283,15 +283,14 @@
     def every(count, body):
         lax.fori_loop(0, count, lambda i, c: (body(i), c)[1], 0)
 
-    mine = pl.ds(pl.multiple_of(me * tokens, tokens), tokens)
     loads = [
         pltpu.make_async_copy(src, dst, load_sem.at[i])
         for i, (src, dst) in enumerate(
             (
                 (st_hbm, st_ref),
                 (x_hbm, x_ref),
-                (bc_ref.at[quad, :, 0:width], b_buf.at[mine, :]),
-                (bc_ref.at[quad, :, width : 2 * width], c_buf.at[mine, :]),
+                (bc_ref.at[quad, :, 0:width], chunk(0, quad, spot)),
+                (bc_ref.at[quad, :, width : 2 * width], chunk(1, quad, spot)),
                 (z_hbm, z_ref),
             )
         )
@@ -368,104 +367,67 @@
             log_gap = turned[:, h : h + 1] - cum_row
             pair[2 * j + h] = jnp.exp(jnp.where(causal, log_gap, -jnp.inf)) * step_row
 
-    loads[1].wait()
-    every(blocks, prepare)
-    loads[2].wait()
-    loads[3].wait()
-    loads[4].wait()
-
-    def gather(k, work):
-        def turn(i):
-            @pl.when(i < quads)
+    for load in loads[1:]:
+        load.wait()
+
+    side_lag, work_lag = 3, 5
+
+    def turn(t):
+        @pl.when(t < 2 * quads)
+        def _():
+            k, i = t // quads, t % quads
+            q = nth(i)
+
+            @pl.when(i > 0)
             def _():
-                q = nth(i)
-
-                @pl.when(i > 0)
-                def _():
-                    near_in(k, q).wait_recv()
-
-                to_side(k, q, spot).start()
-                to_twin(k, q, spot).start()
-                if k == 0:
-
-                    @pl.when(i > 0)
-                    def _():
-                        near(1, q).start()
-
-            @pl.when((i >= 1) & (i < quads + 1))
+                near_in(k, q).wait_recv()
+
+            to_side(k, q, spot).start()
+            to_twin(k, q, spot).start()
+
+            @pl.when((t > 0) & (t < quads))
             def _():
-                q = nth(i - 1)
-                to_side(k, q, side_spot).wait_recv()
-                to_twin_last(k, q, side_spot).start()
-
-            @pl.when(i >= 2)
+                near(1, q).start()
+
+            @pl.when(t < quads)
             def _():
-                q = nth(i - 2)
-                to_twin(k, q, twin_spot).wait_recv()
-                to_twin_last(k, q, diag_spot).wait_recv()
-                work(2 * q)
-                work(2 * q + 1)
-
-        every(quads + 2, turn)
+                prepare(2 * q)
+                prepare(2 * q + 1)
+
+        @pl.when((t >= side_lag) & (t < 2 * quads + side_lag))
+        def _():
+            u = t - side_lag
+            k, q = u // quads, nth(u % quads)
+            to_side(k, q, side_spot).wait_recv()
+            to_twin_last(k, q, side_spot).start()
+
+        @pl.when(t >= work_lag)
+        def _():
+            u = t - work_lag
+            k, q = u // quads, nth(u % quads)
+            to_twin(k, q, twin_spot).wait_recv()
+            to_twin_last(k, q, diag_spot).wait_recv()
+
+            @pl.when(u < quads)
+            def _():
+                add_block(2 * q)
+                add_block(2 * q + 1)
+
+            @pl.when(u >= quads)
+            def _():
+                out_block(2 * q)
+                out_block(2 * q + 1)
 
     def add_block(j):
-        added[j] = rows_dot(carried[rows_of(j), :], b_buf[rows_of(j), :])
-
-    gather(0, add_block)
-
-    every(devices - 1, lambda i: init_from((me + 1 + i) % devices).wait_recv())
-    for k in range(owners):
-        for q in range(8):
-            piece = s_in[8 * k + q].astype(jnp.float32)
-            seeds[k, 8 * q : 8 * q + 8, :] = piece[0:8]
-            seeds[k, 64 + 8 * q : 72 + 8 * q, :] = piece[8:16]
-
-    first = [
-        sum(
-            jnp.where(ps_ref[d] < ps_ref[c], tb_ref[d], 0) for d in range(owners)
-        )
-        for c in range(owners)
-    ]
-    end = [first[c] + tb_ref[c] for c in range(owners)]
-    state_row = lax.broadcasted_iota(jnp.int32, (L, width), 0)
-
-    def advance(j, state):
-        is_start = sum(jnp.where(first[c] == j, 1, 0) for c in range(owners))
-        owner = sum(
-            jnp.where((first[c] <= j) & (j < end[c]), om_ref[c], 0) for c in range(owners)
-        )
-        owner = jnp.clip(owner, 0, owners - 1)
-        start = jnp.where(is_start > 0, seeds[owner], state)
-        starts[j] = start.astype(jnp.bfloat16)
-        decay = jnp.where(
-            state_row < L // 2,
-            edge_scr[pl.ds(2 * j, 1), 0:1],
-            edge_scr[pl.ds(2 * j + 1, 1), 0:1],
-        )
-        after = decay * start + added[j]
-        added[j] = after
-        return after
-
-    lax.fori_loop(0, blocks, advance, jnp.zeros((L, width), jnp.float32))
-
-    for k in range(owners):
-        last = sum(jnp.where(om_ref[c] == k, end[c] - 1, 0) for c in range(owners))
-        done = added[jnp.clip(last, 0, blocks - 1)]
-        for q in range(8):
-            f_out[8 * k + q] = jnp.concatenate(
-                [done[8 * q : 8 * q + 8], done[64 + 8 * q : 72 + 8 * q]], axis=0
-            ).astype(jnp.bfloat16)
-    every(devices - 1, lambda i: fin_copy((me + 1 + i) % devices).start())
-    f_in[me] = f_out[me]
+        added[j] = rows_dot(carried[rows_of(j), :], buf[rows_of(j), :])
 
     skip_lane = jnp.where(square_lane[0:1] < L // 2, skip_ref[0], skip_ref[1])
-    cols_scr[...] = jnp.zeros((L, L), jnp.float32)
 
     def out_block(j):
         rows = rows_of(j)
-        c_block = c_buf[rows, :]
+        c_block = buf[pl.ds(pl.multiple_of(rows_each + j * L, L), L), :]
         x_block = x_ref[rows, :]
-        scores = lanes_dot(c_block, b_buf[rows, :])
+        scores = lanes_dot(c_block, buf[rows, :])
         parts = [
             jnp.dot(
                 (scores * pair[2 * j + h]).astype(jnp.bfloat16),
@@ -484,11 +446,60 @@
         result = mixed * (z_block / (1.0 + jnp.exp(-z_block)))
         gated[rows, :] = result
         total_square = jnp.sum(result * result, axis=1, keepdims=True)
-        cols_scr[...] = jnp.where(square_lane == j, total_square, cols_scr[...])
-
-    gather(1, out_block)
-
-    sq_out[...] = jnp.transpose(cols_scr[...])[0:blocks]
+        sums_scr[...] = jnp.where(square_lane == j, total_square, sums_scr[...])
+
+    every(quads + work_lag, turn)
+
+    every(devices - 1, lambda i: init_from((me + 1 + i) % devices).wait_recv())
+    for k in range(owners):
+        for q in range(8):
+            piece = s_in[8 * k + q].astype(jnp.float32)
+            seeds[k, 8 * q : 8 * q + 8, :] = piece[0:8]
+            seeds[k, 64 + 8 * q : 72 + 8 * q, :] = piece[8:16]
+
+    first = [
+        sum(
+            jnp.where(ps_ref[d] < ps_ref[c], tb_ref[d], 0) for d in range(owners)
+        )
+        for c in range(owners)
+    ]
+    end = [first[c] + tb_ref[c] for c in range(owners)]
+    state_row = lax.broadcasted_iota(jnp.int32, (L, width), 0)
+
+    def advance(j, state):
+        is_start = sum(jnp.where(first[c] == j, 1, 0) for c in range(owners))
+        owner = sum(
+            jnp.where((first[c] <= j) & (j < end[c]), om_ref[c], 0) for c in range(owners)
+        )
+        owner = jnp.clip(owner, 0, owners - 1)
+        start = jnp.where(is_start > 0, seeds[owner], state)
+        starts[j] = start.astype(jnp.bfloat16)
+        decay = jnp.where(
+            state_row < L // 2,
+            edge_scr[pl.ds(2 * j, 1), 0:1],
+            edge_scr[pl.ds(2 * j + 1, 1), 0:1],
+        )
+        after = decay * start + added[j]
+        added[j] = after
+        return after
+
+    lax.fori_loop(0, blocks, advance, jnp.zeros((L, width), jnp.float32))
+
+    for k in range(owners):
+        last = sum(jnp.where(om_ref[c] == k, end[c] - 1, 0) for c in range(owners))
+        done = added[jnp.clip(last, 0, blocks - 1)]
+        for q in range(8):
+            f_out[8 * k + q] = jnp.concatenate(
+                [done[8 * q : 8 * q + 8], done[64 + 8 * q : 72 + 8 * q]], axis=0
+            ).astype(jnp.bfloat16)
+    every(devices - 1, lambda i: fin_copy((me + 1 + i) % devices).start())
+    f_in[me] = f_out[me]
+
+    sums_scr[...] = jnp.zeros((L, L), jnp.float32)
+
+    lax.fori_loop(quads + work_lag, 2 * quads + work_lag, lambda t, c: (turn(t), c)[1], 0)
+
+    sq_out[...] = jnp.transpose(sums_scr[...])[0:blocks]
 
     def sq_copy(i):
         other = (spot + 1 + i) % 4
@@ -503,7 +514,7 @@
     every(devices - 1, lambda i: fin_from((me + 1 + i) % devices).wait_recv())
 
     def widen(d):
-        ns_ref[pl.ds(pl.multiple_of(d * 16, 16), 16), :] = f_in[d].astype(jnp.float32)
+        ns_ref[pl.ds(pl.multiple_of(d * 16, 16), 16), :] = f_in[d]
 
     every(devices, widen)
     every(3, lambda i: sq_from(i).wait_recv())
@@ -571,7 +582,7 @@
         functools.partial(layer_kernel, devices, blocks, owners),
         out_shape=(
             jax.ShapeDtypeStruct((tokens, columns), bf16),
-            jax.ShapeDtypeStruct((devices * 16, state), f32),
+            jax.ShapeDtypeStruct((devices * 16, state), bf16),
         ),
         in_specs=[smem] * 6 + [vmem] * 2 + [pl.BlockSpec(memory_space=pl.ANY)] * 4,
         out_specs=(vmem, vmem),
@@ -579,8 +590,7 @@
             pltpu.VMEM((tokens, columns), bf16),
             pltpu.VMEM((tokens, columns), bf16),
             pltpu.VMEM((devices * 16, state), f32),
-            pltpu.VMEM((tokens, state), bf16),
-            pltpu.VMEM((tokens, state), bf16),
+            pltpu.VMEM((2 * tokens, state), bf16),
             pltpu.VMEM((devices, 16, state), bf16),
             pltpu.VMEM((devices, 16, state), bf16),
             pltpu.VMEM((devices, 16, state), bf16),
@@ -597,6 +607,7 @@
             pltpu.VMEM((4 * blocks, L), f32),
             pltpu.VMEM((L, L), f32),
             pltpu.VMEM((2 * blocks, L), f32),
+            pltpu.VMEM((L, L), f32),
         ]
         + [dma((2, quads))] * 8
         + [dma((devices,))] * 4
@@ -619,7 +630,7 @@
         bc_in,
         owner_states.reshape(-1, state),
     )
-    return (y_out, new_states.reshape(owner_states.shape))
+    return (y_out, new_states.astype(f32).reshape(owner_states.shape))
 
 
 def choose(*arrays):

time: 59.9 us -> 48.5 us (0.81)
  Pallas kernels: 56.3 us -> 45.1 us
  local copies, waits for them, and re-layouts: 2.72 us -> 0.8 us
  other arithmetic: 0 us -> 1.84 us
    pallas_call x1, Pallas kernels: 56.3 us -> 45.1 us  [fused(): pl.pallas_call(functools.partial(layer_kernel, devices, blocks, owners),...]
    unnamed x4 -> x3, local copies, waits for them, and re-layouts: 2.72 us -> 0.8 us
    reshape x0 -> x1, other arithmetic: none -> 1.84 us  [fused(): return (y_out, new_states.astype(f32).reshape(owner_states.shape))]
where the time goes in v4:
time: 48.5 us; the launch traced here: 48.3 us
  Pallas kernels  45.1 us (93%)
  other arithmetic  1.84 us (4%)
  local copies, waits for them, and re-layouts  0.8 us (2%)
  between operations  0.65 us (1%)
    pallas_call x1, Pallas kernels, fused(): pl.pallas_call(functools.partial(layer_kernel, devices, blocks, owners),...  45.1 us
    reshape x1, other arithmetic, fused(): return (y_out, new_states.astype(f32).reshape(owner_states.shape))  1.84 us

profile of v4, /device:TPU:0, one launch (start us, length us, event | category | flops | bytes accessed | tf_op | source)
XLA Modules:
  0.0 48.3 jit_solution(12495613865855957752)
XLA Ops:
  0.6 45.1 %shard_map.131 = (bf16[2048,128]{1,0:T(8,128)(2,1)}, bf16[512,256]{1,0:T(8,128)(2,1)}) custom-call(s32[4]{0:T(128)} %om_ref.1, s32[4]{0:T(128)} %ps_ref.1, s32[4]{0:T(128)} %tb_ref.1, f32[2]{0:T(128)} %bias_ref.1, f32[2]{0:T(128)} %rate_ref.1, f32[2]{0:T(128)} %skip_ref.1, bf16[2,2048]{1,0:T(2,128)(2,1)} %dt_ref.1, f32[1,128]{1,0:T(1,128)} %bitcast.6, ...), custom_call_target="tpu_custom_call" | custom-call | tf_op jit(solution)/shard_map/pallas_call | solution.py:581
  45.7 0.0 copy-start
  45.7 1.8 %bitcast_convert_fusion = f32[1,1,64,8,256]{4,3,2,1,0:T(8,128)} fusion(bf16[512,256]{1,0:T(8,128)(2,1)} %get-tuple-element.5), kind=kLoop, calls=%fused_computation | loop fusion | flops 131072 | bytes 786432 | tf_op jit(solution)/shard_map/reshape | solution.py:633
  47.5 0.0 copy-done
  47.5 0.8 %copy.15 = bf16[2048,128]{1,0:T(8,128)(2,1)} copy(bf16[2048,128]{1,0:T(8,128)(2,1)S(1)} %copy-done) | data formatting | bytes 1048576
Async XLA Ops:
  45.7 1.8 %copy-start = (bf16[2048,128]{1,0:T(8,128)(2,1)S(1)}, bf16[2048,128]{1,0:T(8,128)(2,1)}, u32[]{:S(2)}) copy-start(bf16[2048,128]{1,0:T(8,128)(2,1)} %get-tuple-element.8) | copy-start | bytes 1572868

commit v5 on v4

--- a/solution.py
+++ b/solution.py
@@ -370,7 +370,7 @@
     for load in loads[1:]:
         load.wait()
 
-    side_lag, work_lag = 3, 5
+    side_lag, work_lag = 5, 8
 
     def turn(t):
         @pl.when(t < 2 * quads)

time: 48.5 us -> 47.2 us (0.973)
  Pallas kernels: 45.1 us -> 43.8 us
    pallas_call x1, Pallas kernels: 45.1 us -> 43.8 us  [fused(): pl.pallas_call(functools.partial(layer_kernel, devices, blocks, owners),...]
where the time goes in v5:
time: 47.2 us; the launch traced here: 47 us
  Pallas kernels  43.8 us (93%)
  other arithmetic  1.84 us (4%)
  local copies, waits for them, and re-layouts  0.8 us (2%)
  between operations  0.65 us (1%)
    pallas_call x1, Pallas kernels, fused(): pl.pallas_call(functools.partial(layer_kernel, devices, blocks, owners),...  43.8 us
    reshape x1, other arithmetic, fused(): return (y_out, new_states.astype(f32).reshape(owner_states.shape))  1.84 us

profile of v5, /device:TPU:0, one launch (start us, length us, event | category | flops | bytes accessed | tf_op | source)
XLA Modules:
  0.0 47.0 jit_solution(15283353923112716524)
XLA Ops:
  0.6 43.8 %shard_map.131 = (bf16[2048,128]{1,0:T(8,128)(2,1)}, bf16[512,256]{1,0:T(8,128)(2,1)}) custom-call(s32[4]{0:T(128)} %om_ref.1, s32[4]{0:T(128)} %ps_ref.1, s32[4]{0:T(128)} %tb_ref.1, f32[2]{0:T(128)} %bias_ref.1, f32[2]{0:T(128)} %rate_ref.1, f32[2]{0:T(128)} %skip_ref.1, bf16[2,2048]{1,0:T(2,128)(2,1)} %dt_ref.1, f32[1,128]{1,0:T(1,128)} %bitcast.6, ...), custom_call_target="tpu_custom_call" | custom-call | tf_op jit(solution)/shard_map/pallas_call | solution.py:581
  44.4 0.0 copy-start
  44.4 1.8 %bitcast_convert_fusion = f32[1,1,64,8,256]{4,3,2,1,0:T(8,128)} fusion(bf16[512,256]{1,0:T(8,128)(2,1)} %get-tuple-element.5), kind=kLoop, calls=%fused_computation | loop fusion | flops 131072 | bytes 786432 | tf_op jit(solution)/shard_map/reshape | solution.py:633
  46.2 0.0 copy-done
  46.2 0.8 %copy.15 = bf16[2048,128]{1,0:T(8,128)(2,1)} copy(bf16[2048,128]{1,0:T(8,128)(2,1)S(1)} %copy-done) | data formatting | bytes 1048576
Async XLA Ops:
  44.4 1.8 %copy-start = (bf16[2048,128]{1,0:T(8,128)(2,1)S(1)}, bf16[2048,128]{1,0:T(8,128)(2,1)}, u32[]{:S(2)}) copy-start(bf16[2048,128]{1,0:T(8,128)(2,1)} %get-tuple-element.8) | copy-start | bytes 1572868
